TPU v7x, 256 devices: a whole 4x4x8 slice. The times are simulated.
256 devices in a mesh: group: 2 (over z_hi), dp: 8 (over x, core), tensor: 16 (over z_lo, y).
Axes of the slice: x: 4, y: 4, z: 8 (z_hi: 2, z_lo: 4; z = z_hi * 4 + z_lo), core: 2. Of those that a mesh axis runs over, the one named last changes fastest.
Arguments:
- teacher_hidden: bfloat16 [4096, 8192], P(('group', 'dp'), 'tensor'), may hold values from -6 to 6
- teacher_gain: float32 [8192], P('tensor'), may hold values from 0.1 to 1.9
- project_weight: bfloat16 [8192, 3584], P('tensor'), may hold values from -0.0625 to 0.0625
- student_hidden: bfloat16 [4096, 3584], P(('group', 'dp', 'tensor')), may hold values from -6 to 6
- student_gain: float32 [3584], replicated, may hold values from 0.1 to 1.9
- gate_weight: bfloat16 [3584, 9472], P(('group', 'dp'), 'tensor'), may hold values from -0.09375 to 0.09375
- up_weight: bfloat16 [3584, 9472], P(('group', 'dp'), 'tensor'), may hold values from -0.09375 to 0.09375
- down_weight: bfloat16 [9472, 3584], P('tensor', ('group', 'dp')), may hold values from -0.0625 to 0.0625
- owner_map: int32 [256, 1], P(('group', 'dp')), may hold values from 0 to 15; in each aligned block of 16 rows (0 to 15, 16 to 31, ...) at most 2 rows name the same one
- token_ids: int32 [4096], P(('group', 'dp', 'tensor')), may hold values from 0 to 511
- token_counts: int32 [256], P(('group', 'dp')), may hold values from 1 to 16
- id_weight: float32 [512], replicated, may hold values from 0.25 to 4
Outputs:
- student_out: bfloat16 [16, 16, 32, 3584], P(('group', 'dp'), 'tensor')
- down_grad: float32 [3584, 9472], P(('group', 'dp'), 'tensor')
Inputs may be any that keep to these rules, and one draw needn't show every extreme that they name: `owner_map`: of the 16 episodes of one index of group and dp (aligned blocks of 16 rows), at most 2 have the same owner; owner o is index o of group and dp in mesh order.
All inputs are finite; a program needn't handle non-finite values.
Results may differ from a plain program's by a relative error of at most 0.02.
Values may be sent and summed in bfloat16 or wider, within the bound.
No kernel may reach another device: no remote copies, remote signals or barrier semaphores. Data moves between devices by JAX's collectives and lax.ppermute only.
A program may use at most 128 MiB of HBM per device.

v0:
```python
import math
import jax
import jax.numpy as jnp
from jax import lax
from jax.sharding import Mesh
from jax.sharding import PartitionSpec as P

DT = 8192
EP_LEN = 16
TENSOR = ("tensor_0", "tensor_1")
GROUP_DP_TENSOR = ("group", "dp", "tensor_0", "tensor_1")
EPSILON = 1e-06


def side_by_side(arrays, axis, split_dim, concat_dim, along):
    columns = [a.reshape(*a.shape[:along], -1) for a in arrays]
    both = jnp.concatenate(columns, axis=along)
    result, at, finished = (
        lax.all_to_all(both, axis, split_axis=split_dim, concat_axis=concat_dim, tiled=True),
        0,
        [],
    )
    for a, column in zip(arrays, columns):
        slab = result[..., at : at + column.shape[along]]
        finished.append(slab.reshape(*slab.shape[:along], *a.shape[along:]))
        at += column.shape[along]
    return tuple(finished)


def copy_for_each(array, axis):
    devices = lax.axis_size(axis)
    return lax.all_to_all(
        jnp.broadcast_to(array[None], (devices, *array.shape)), axis, 0, 0, tiled=True
    )


def of_everyone(array, axis):
    return copy_for_each(array, axis).sum(axis=0)


def joined_along(tiles, dim):
    tiles = jnp.moveaxis(tiles, 0, dim)
    shape = tiles.shape
    return tiles.reshape(*shape[:dim], shape[dim] * shape[dim + 1], *shape[dim + 2 :])


def all_blocks(array, axes, turns):
    tiles = array
    for k in turns:
        tiles = lax.all_gather(tiles, axes[k])
    done = turns[::-1]
    back = [done.index(k) for k in range(len(axes))]
    tiles = tiles.transpose(*back, *range(len(axes), tiles.ndim))
    return tiles.reshape(-1, *array.shape)


def gather_axes(array, axes, turns, dim):
    return joined_along(all_blocks(array, axes, turns), dim)


def sent_together(arrays, axis, dim, along):
    both = jnp.concatenate(arrays, axis=along)
    result, at, finished = (lax.all_gather(both, axis, axis=dim, tiled=True), 0, [])
    for a in arrays:
        finished.append(lax.slice_in_dim(result, at, at + a.shape[along], axis=along))
        at += a.shape[along]
    return tuple(finished)


def build_selector(owner_local, owners, capacity):
    owner_list = owner_local[:, 0]
    onehot = (owner_list[:, None] == jnp.arange(owners, dtype=jnp.int32)[None, :]).astype(jnp.int32)
    earlier = jnp.cumsum(onehot, axis=0) - onehot
    rank_list = jnp.sum(earlier * onehot, axis=1)
    target = owner_list * capacity + rank_list
    return (target[None, :] == jnp.arange(owners * capacity, dtype=jnp.int32)[:, None]).astype(
        jnp.bfloat16
    )


def dispatch_rows(selector, values):
    return jnp.einsum("re,pef->prf", selector, values, preferred_element_type=jnp.float32).astype(
        jnp.bfloat16
    )


def dispatch_plain(selector, values):
    return jnp.einsum("re,pe->pr", selector, values, preferred_element_type=jnp.float32).astype(
        jnp.bfloat16
    )


def regroup_rows(payload):
    return (
        lax.all_to_all(payload[0], ("group", "dp"), split_axis=1, concat_axis=1, tiled=True),
        *side_by_side((payload[1], payload[2]), ("group", "dp"), 1, 1, 2),
    )


def teacher_scaling(raw_rows, teacher_gain):
    widened = raw_rows.astype(jnp.float32)
    return (
        jnp.sum(widened * widened, axis=1),
        (widened * teacher_gain[None, :]).astype(jnp.bfloat16),
    )


def local(
    teacher_hidden,
    teacher_gain,
    project_weight,
    student_hidden,
    student_gain,
    gate_weight,
    up_weight,
    down_weight,
    owner_map,
    token_ids,
    token_counts,
    id_weight,
):
    groups = lax.axis_size("group")
    places = lax.axis_size("dp")
    owners = groups * places
    tensors = lax.axis_size(TENSOR)
    tensor_index = lax.axis_index(TENSOR)
    episodes = token_counts.shape[0]
    own_span = EP_LEN // tensors
    capacity = max(2, 2 * episodes // owners)
    received = owners * capacity
    student_width = student_hidden.shape[1]
    selector = build_selector(owner_map, owners, capacity)
    id_rows = token_ids.reshape(own_span, episodes)
    looked = jnp.sum(
        jnp.where(
            id_rows[:, :, None] == jnp.arange(id_weight.shape[0], dtype=jnp.int32)[None, None, :],
            id_weight[None, None, :],
            0.0,
        ),
        axis=2,
    )
    position = tensor_index * own_span + jnp.arange(own_span, dtype=jnp.int32)[:, None]
    token_weight = jnp.where(position < token_counts[None, :], looked, 0.0).astype(jnp.bfloat16)
    sent_weight = dispatch_plain(selector, token_weight)
    sent_student = dispatch_rows(
        selector, student_hidden.reshape(own_span, episodes, student_width)
    )
    sent_raw = dispatch_rows(selector, teacher_hidden.reshape(EP_LEN, episodes, -1))
    arrived = regroup_rows((sent_raw, sent_student, sent_weight))
    squares, scaled = teacher_scaling(arrived[0].reshape(EP_LEN * received, -1), teacher_gain)
    totals = of_everyone(squares, TENSOR)
    inverse = lax.rsqrt(totals / DT + EPSILON)
    share_rows = own_span * received
    summed = lax.psum_scatter(
        jnp.dot(scaled, project_weight, preferred_element_type=jnp.float32).astype(jnp.bfloat16),
        TENSOR,
        scatter_dimension=0,
        tiled=True,
    ).astype(jnp.float32)
    own_inverse = lax.dynamic_slice_in_dim(inverse, tensor_index * share_rows, share_rows, 0)
    teacher_mine = (
        (summed * own_inverse[:, None])
        .astype(jnp.bfloat16)
        .reshape(own_span, received, student_width)
    )
    student_block = arrived[1].reshape(own_span * received, student_width).astype(jnp.float32)
    rescale = lax.rsqrt(jnp.mean(student_block * student_block, axis=1, keepdims=True) + EPSILON)
    normed = (student_block * rescale * student_gain[None, :]).astype(jnp.bfloat16)
    gathered = gather_axes(normed, TENSOR, (0, 1), 0)
    pieces = sent_together((gate_weight, up_weight), ("group", "dp"), 0, 1)
    gate_sum = jnp.dot(gathered, pieces[0], preferred_element_type=jnp.float32)
    up_sum = jnp.dot(gathered, pieces[1], preferred_element_type=jnp.float32)
    activated = (jax.nn.silu(gate_sum) * up_sum).astype(jnp.bfloat16)
    branch = jnp.dot(
        activated,
        lax.all_gather(down_weight, ("group", "dp"), axis=1, tiled=True),
        preferred_element_type=jnp.float32,
    )
    branch_local = lax.psum_scatter(
        branch.astype(jnp.bfloat16), TENSOR, scatter_dimension=0, tiled=True
    ).astype(jnp.float32)
    predicted = student_block + branch_local
    student_out = predicted.astype(jnp.bfloat16).reshape(1, own_span, received, student_width)
    difference = predicted - teacher_mine.reshape(-1, student_width).astype(jnp.float32)
    weight_rows = arrived[2].reshape(-1, 1).astype(jnp.float32)
    tokens_all = EP_LEN * episodes * owners
    grad_block = (weight_rows * difference * (1.0 / math.sqrt(tokens_all))).astype(jnp.bfloat16)
    grad_all = gather_axes(grad_block, TENSOR, (0, 1), 0)
    down_grad = lax.psum_scatter(
        jnp.einsum("rc,rh->ch", grad_all, activated, preferred_element_type=jnp.float32).astype(
            jnp.bfloat16
        ),
        ("group", "dp"),
        scatter_dimension=0,
        tiled=True,
    ).astype(jnp.float32)
    return (student_out, down_grad)


def solution(mesh):
    split = Mesh(
        mesh.devices.reshape(mesh.shape["group"], mesh.shape["dp"], 4, 4),
        ("group", "dp", "tensor_0", "tensor_1"),
    )
    placed = (
        P(("group", "dp"), TENSOR),
        P(TENSOR),
        P(TENSOR, None),
        P(GROUP_DP_TENSOR, None),
        P(),
        P(("group", "dp"), TENSOR),
        P(("group", "dp"), TENSOR),
        P(TENSOR, ("group", "dp")),
        P(("group", "dp"), None),
        P(GROUP_DP_TENSOR),
        P(("group", "dp")),
        P(),
    )
    return jax.shard_map(
        local,
        mesh=split,
        in_specs=placed,
        out_specs=(P(("group", "dp"), TENSOR, None, None), P(("group", "dp"), TENSOR)),
        check_vma=False,
    )
```

profile of v0, /device:TPU:8, one launch (start us, length us, event | category | flops | bytes accessed | tf_op | source)
XLA Modules:
  0.0 588.3 jit_solution(2817465092216490723)
XLA Ops:
  8.1 0.7 fusion.24
  8.8 0.8 select_reduce_fusion.1
  9.7 0.7 multiply_add_fusion
  10.3 0.9 select_reduce_fusion
  11.2 0.8 fusion.13
  12.1 0.1 copy.39
  12.2 1.2 fusion.4
  13.4 0.4 copy.54
  13.8 0.5 broadcast.101
  14.3 2.1 reduce.5
  16.4 0.1 reshape.162
  16.5 22.6 %all_to_all.16 = bf16[16,2,3585]{2,1,0:T(2,128)(2,1)S(1)} all-to-all(bf16[16,2,3585]{2,1,0:T(2,128)(2,1)S(1)} %reshape.162), channel_id=1, replica_groups=mesh['group'=2,'dp'=8,'tensor_0'=4,'tensor_1'=4] {'group','dp'}, dimensions={0} | all-to-all | bytes 458880 | tf_op jit(solution)/shard_map/all_to_all | solution.py:19
  39.2 0.2 reshape.163
  39.4 0.5 slice.16
  39.9 0.2 fusion.17
  40.1 0.1 fusion.19
  40.2 21.6 %all_gather.28 = bf16[4,32,3584]{2,1,0:T(8,128)(2,1)} all-gather(bf16[1,32,3584]{2,1,0:T(8,128)(2,1)S(1)} %fusion.19), channel_id=1, replica_groups=mesh['group'=2,'dp'=8,'tensor_0'=4,'tensor_1'=4] {'tensor_0'}, dimensions={0}, use_global_device_ids=true | all-gather | bytes 1146880 | tf_op jit(solution)/shard_map/all_gather | solution.py:50
  61.9 1.0 pad_maximum_fusion
  62.9 0.7 all-gather.10.cloned.1.call-update
  63.7 0.4 fusion.11
  64.1 0.3 copy.43
  64.4 19.4 %all_to_all.17 = bf16[16,32,512]{2,0,1:T(8,128)(2,1)S(1)} all-to-all(bf16[16,32,512]{2,0,1:T(8,128)(2,1)S(1)} %copy.43), channel_id=1, replica_groups=mesh['group'=2,'dp'=8,'tensor_0'=4,'tensor_1'=4] {'group','dp'}, dimensions={1} | all-to-all | bytes 1048576 | tf_op jit(solution)/shard_map/all_to_all | solution.py:95
  83.8 0.3 copy_convert_fusion
  84.2 0.1 fusion.14
  84.3 3.9 convolution_convert_fusion.1
  88.2 0.2 reduce-scatter.4.cloned.1.call-start
  88.4 15.2 %all-gather.12.cloned.1.call-done = bf16[16,32,3584]{2,1,0:T(8,128)(2,1)} async-done(((bf16[4,32,3584]{2,1,0:T(8,128)(2,1)}), bf16[16,32,3584]{2,1,0:T(8,128)(2,1)}) %all-gather.12.cloned.1.call-update) | async-done | bytes 3670032 | tf_op jit(solution)/shard_map/all_gather | solution.py:50
  103.6 4.2 copy.42
  107.8 116.3 %all-gather.8.cloned.1.call-done = bf16[3584,1184]{1,0:T(8,128)(2,1)} async-done(((bf16[224,1184]{1,0:T(8,128)(2,1)}), bf16[3584,1184]{1,0:T(8,128)(2,1)}) %all-gather.8.cloned.1.call-update) | async-done | bytes 8486928 | tf_op jit(solution)/shard_map/all_gather | solution.py:63
  224.1 6.0 %fusion.2 = f32[512,592]{0,1:T(8,128)S(1)} fusion(bf16[512,3584]{1,0:T(8,128)(2,1)} %bitcast.71, bf16[3584,1184]{1,0:T(8,128)(2,1)} %all-gather.8.cloned.1.call-done), kind=kOutput, calls=%fused_computation.5 | convolution fusion | flops 2172649472 | bytes 9469952 | tf_op jit(solution)/shard_map/dot_general | solution.py:171
  230.2 1.2 copy-done.6
  231.3 4.2 fusion.8
  235.6 71.2 %all-gather.10.cloned.1.call-done = bf16[592,3584]{0,1:T(8,128)(2,1)} async-done(((bf16[592,224]{0,1:T(8,128)(2,1)}), bf16[592,3584]{0,1:T(8,128)(2,1)}) %all-gather.10.cloned.1.call-update) | async-done | bytes 4243472 | tf_op jit(solution)/shard_map/all_gather | solution.py:176
  306.8 6.9 %convolution_convert_fusion.2 = bf16[512,3584]{1,0:T(8,128)(2,1)} fusion(bf16[512,592]{0,1:T(8,128)(2,1)S(1)} %fusion.8, bf16[592,3584]{0,1:T(8,128)(2,1)} %all-gather.10.cloned.1.call-done), kind=kOutput, calls=%fused_computation.2 | convolution fusion | flops 2174484480 | bytes 8519680 | tf_op jit(solution)/shard_map/dot_general | solution.py:174
  313.7 0.4 multiply_reduce_fusion
  314.1 0.1 broadcast_in_dim.23
  314.2 0.6 broadcast_in_dim.38
  314.8 5.0 all-to-all-start.2
  319.9 0.3 fusion.22
  320.2 6.8 %all-to-all-done.2 = f32[16,1,512]{2,1,0:T(1,128)S(1)} async-done(((f32[16,1,512]{2,1,0:T(1,128)}), f32[16,1,512]{2,1,0:T(1,128)S(1)}, u32[]{:S(2)}, u32[]{:S(2)}) %all-to-all-start.2) | async-done | bytes 32800 | tf_op jit(solution)/shard_map/all_to_all | solution.py:32
  327.1 70.7 %reduce-scatter.4.cloned.1.call-done = bf16[32,3584]{1,0:T(8,128)(2,1)} async-done(((bf16[512,3584]{1,0:T(8,128)(2,1)}), bf16[32,3584]{1,0:T(8,128)(2,1)}) %reduce-scatter.4.cloned.1.call-update) | async-done | bytes 229392 | tf_op jit(solution)/shard_map/reduce_scatter | solution.py:179
  397.8 1.9 multiply_convert_fusion
  399.7 16.8 %all-gather.1 = bf16[128,3584]{1,0:T(8,128)(2,1)} all-gather(bf16[32,3584]{1,0:T(8,128)(2,1)S(1)} %get-tuple-element.4), channel_id=3, replica_groups=mesh['group'=2,'dp'=8,'tensor_0'=4,'tensor_1'=4] {'tensor_0'}, dimensions={0}, use_global_device_ids=true | all-gather | bytes 1146880 | tf_op jit(solution)/shard_map/all_gather | solution.py:50
  416.6 47.2 %all-gather.14.cloned.1.call-done = bf16[16,32,3584]{2,1,0:T(8,128)(2,1)} async-done(((bf16[4,32,3584]{2,1,0:T(8,128)(2,1)}), bf16[16,32,3584]{2,1,0:T(8,128)(2,1)}) %all-gather.14.cloned.1.call-update) | async-done | bytes 3670032 | tf_op jit(solution)/shard_map/all_gather | solution.py:50
  463.7 2.3 copy.46
  466.0 4.7 convolution_convert_fusion
  470.7 108.7 %reduce-scatter.8.cloned.1.call-done = bf16[224,592]{1,0:T(8,128)(2,1)} async-done(((bf16[3584,592]{1,0:T(8,128)(2,1)}), bf16[224,592]{1,0:T(8,128)(2,1)}) %reduce-scatter.8.cloned.1.call-update) | async-done | bytes 265232 | tf_op jit(solution)/shard_map/reduce_scatter | solution.py:189
  579.4 1.8 convert_element_type.128
  (34 shorter events, 0.6 us)
Async XLA Ops:
  8.0 55.7 %copy-start = (bf16[256,512]{1,0:T(8,128)(2,1)S(1)}, bf16[256,512]{1,0:T(8,128)(2,1)}, u32[]{:S(2)}) copy-start(bf16[256,512]{1,0:T(8,128)(2,1)} %param.12) | copy-start | bytes 786436
  8.0 32.0 %copy-start.4 = (f32[3584]{0:T(1024)S(1)}, f32[3584]{0:T(1024)}, u32[]{:S(2)}) copy-start(f32[3584]{0:T(1024)} %param.16) | copy-start | bytes 43012
  8.0 95.6 %all-gather.12.cloned.1.call-start = ((), (), s32[]{:S(2)}) async-start(), calls=%async_computation.11 | async-start | bytes 4587520 | tf_op jit(solution)/shard_map/all_gather | solution.py:50
  13.4 48.5 %copy-start.2 = (bf16[224,592]{1,0:T(8,128)(2,1)S(1)}, bf16[224,592]{1,0:T(8,128)(2,1)}, u32[]{:S(2)}) copy-start(bf16[224,592]{1,0:T(8,128)(2,1)} %param.18) | copy-start | bytes 795652
  13.4 48.5 %copy-start.3 = (bf16[224,592]{1,0:T(8,128)(2,1)S(1)}, bf16[224,592]{1,0:T(8,128)(2,1)}, u32[]{:S(2)}) copy-start(bf16[224,592]{1,0:T(8,128)(2,1)} %param.17) | copy-start | bytes 795652
  61.8 22.3 %copy-start.5 = (f32[512]{0:T(512)S(1)}, f32[512]{0:T(512)}, u32[]{:S(2)}) copy-start(f32[512]{0:T(512)} %param.13) | copy-start | bytes 6148
  61.8 162.3 %all-gather.8.cloned.1.call-start = ((), (), s32[]{:S(2)}) async-start(), calls=%async_computation.6 | async-start | bytes 9748480 | tf_op jit(solution)/shard_map/all_gather | solution.py:63
  62.9 243.9 %all-gather.10.cloned.1.call-start = ((), (), s32[]{:S(2)}) async-start(), calls=%async_computation.7 | async-start | bytes 4874240 | tf_op jit(solution)/shard_map/all_gather | solution.py:176
  63.6 263.4 %reduce-scatter.6.cloned.1.call-start = ((), (), s32[]{:S(2)}) async-start(), calls=%async_computation.9 | async-start | bytes 3899392 | tf_op jit(solution)/shard_map/reduce_scatter | solution.py:154
  63.7 20.6 %copy-start.7 = (bf16[512,3584]{1,0:T(8,128)(2,1)S(1)}, bf16[512,3584]{1,0:T(8,128)(2,1)}, u32[]{:S(2)}) copy-start(bf16[512,3584]{1,0:T(8,128)(2,1)} %param.14) | copy-start | bytes 11010052
  88.2 309.6 %reduce-scatter.4.cloned.1.call-start = ((), (), s32[]{:S(2)}) async-start(), calls=%async_computation.8 | async-start | bytes 3899392 | tf_op jit(solution)/shard_map/reduce_scatter | solution.py:179
  224.1 6.0 %copy-start.1 = (bf16[4,4,32,3584]{3,2,1,0:T(8,128)(2,1)S(1)}, bf16[4,4,32,3584]{3,2,1,0:T(8,128)(2,1)}, u32[]{:S(2)}) copy-start(bf16[4,4,32,3584]{3,2,1,0:T(8,128)(2,1)} %copy.42) | copy-start | bytes 11010052
  224.1 7.2 %copy-start.6 = (bf16[3584,1184]{1,0:T(8,128)(2,1)S(1)}, bf16[3584,1184]{1,0:T(8,128)(2,1)}, u32[]{:S(2)}) copy-start(bf16[3584,1184]{1,0:T(8,128)(2,1)} %all-gather.8.cloned.1.call-done) | copy-start | bytes 25460740
  314.8 12.1 %all-to-all-start.2 = ((f32[16,1,512]{2,1,0:T(1,128)}), f32[16,1,512]{2,1,0:T(1,128)S(1)}, u32[]{:S(2)}, u32[]{:S(2)}) async-start(f32[16,1,512]{2,1,0:T(1,128)} %broadcast_in_dim.38), calls=%async_computation.4 | async-start | bytes 65536 | tf_op jit(solution)/shard_map/all_to_all | solution.py:32
  319.8 143.9 %all-gather.14.cloned.1.call-start = ((), (), s32[]{:S(2)}) async-start(), calls=%async_computation.12 | async-start | bytes 4587520 | tf_op jit(solution)/shard_map/all_gather | solution.py:50
  416.5 162.9 %reduce-scatter.8.cloned.1.call-start = ((), (), s32[]{:S(2)}) async-start(), calls=%async_computation.10 | async-start | bytes 4874240 | tf_op jit(solution)/shard_map/reduce_scatter | solution.py:189
Sparse Core Ops, SparseCore 0:
  62.0 41.6 all-gather.11
  106.9 117.1 all-gather.7
  226.9 79.9 all-gather.9
  416.6 47.0 all-gather.13
  470.9 108.4 reduce-scatter.7
Sparse Core Ops, SparseCore 1:
  88.3 145.6 reduce-scatter.5
  313.8 83.9 reduce-scatter.3
where the time goes:
time: 589 us; the launch traced here: 588 us
  waiting for transfers between devices  437 us (74%)
  blocking collectives  80.5 us (14%)
  matrix products  28.2 us (5%)
  between operations  15.4 us (3%)
  other arithmetic  11.4 us (2%)
  local copies, waits for them, and re-layouts  10.5 us (2%)
    all_gather x1, waiting for transfers between devices, sent_together(): lax.all_gather(both, axis, axis=dim, tiled=True)  116 us
    reduce_scatter x1, waiting for transfers between devices, local(): lax.psum_scatter(jnp.einsum('rc,rh->ch', grad_all, activated, preferred_e...  109 us
    all_gather x1, waiting for transfers between devices, local(): lax.all_gather(down_weight, ('group', 'dp'), axis=1, tiled=True)  71.2 us
    reduce_scatter x1, waiting for transfers between devices, local(): lax.psum_scatter(branch.astype(jnp.bfloat16), TENSOR, scatter_dimension=0...  70.7 us
    all_gather x2, waiting for transfers between devices, all_blocks(): tiles = lax.all_gather(tiles, axes[k])  62.4 us
    all_gather x2, blocking collectives, all_blocks(): tiles = lax.all_gather(tiles, axes[k])  38.4 us
    all_to_all x1, blocking collectives, side_by_side(): lax.all_to_all(both, axis, split_axis=split_dim, concat_axis=concat_dim,...  22.6 us
    all_to_all x1, blocking collectives, regroup_rows(): lax.all_to_all(payload[0], ('group', 'dp'), split_axis=1, concat_axis=1,...  19.4 us
  transfers between devices with their start and end apart: 8, of which 7 were waited for; matrix products, arithmetic and copies ran while one was open for 5% of the time, Pallas kernels for 0%

commit v1 on v0

--- a/solution.py
+++ b/solution.py
@@ -171,10 +171,12 @@
     gate_sum = jnp.dot(gathered, pieces[0], preferred_element_type=jnp.float32)
     up_sum = jnp.dot(gathered, pieces[1], preferred_element_type=jnp.float32)
     activated = (jax.nn.silu(gate_sum) * up_sum).astype(jnp.bfloat16)
+    carry_figure = lambda w_in, peer_axis: jnp.concatenate(
+        lax.all_to_all(jnp.stack([w_in for _ in range(lax.axis_size(peer_axis))]), peer_axis, 0, 0),
+        axis=1,
+    )
     branch = jnp.dot(
-        activated,
-        lax.all_gather(down_weight, ("group", "dp"), axis=1, tiled=True),
-        preferred_element_type=jnp.float32,
+        activated, carry_figure(down_weight, ("group", "dp")), preferred_element_type=jnp.float32
     )
     branch_local = lax.psum_scatter(
         branch.astype(jnp.bfloat16), TENSOR, scatter_dimension=0, tiled=True

time: 589 us -> 605 us (1.027)
  starting transfers between devices: 5.48 us -> 28.3 us
  waiting for transfers between devices: 437 us -> 426 us
    all_gather x1 -> x0, waiting for transfers between devices: 71.2 us -> none  [local(): lax.all_gather(down_weight, ('group', 'dp'), axis=1, tiled=True)]
    all_gather x1, waiting for transfers between devices: 116 us -> 173 us  [sent_together(): lax.all_gather(both, axis, axis=dim, tiled=True)]
    all_to_all x1, starting transfers between devices: 5.01 us -> 23.1 us  [copy_for_each(): lax.all_to_all(jnp.broadcast_to(array[None], (devices, *array.shape)), ax...]
    reduce_scatter x1, waiting for transfers between devices: 70.7 us -> 84.2 us  [local(): lax.psum_scatter(branch.astype(jnp.bfloat16), TENSOR, scatter_dimension=0...]
    all_gather x2, waiting for transfers between devices: 62.4 us -> 53.9 us  [all_blocks(): tiles = lax.all_gather(tiles, axes[k])]
  transfers between devices with their start and end apart: 8 -> 8, of which waited for: 7 -> 6; matrix products, arithmetic and copies ran while one was open for 5% -> 5% of each run, Pallas kernels for 0% -> 0%
where the time goes in v1:
time: 605 us
  waiting for transfers between devices  426 us (70%)
  blocking collectives  80.3 us (13%)
  matrix products  30.2 us (5%)
  starting transfers between devices  28.3 us (5%)
  between operations  15.4 us (3%)
  local copies, waits for them, and re-layouts  12.9 us (2%)
  other arithmetic  11.4 us (2%)
    all_gather x1, waiting for transfers between devices, sent_together(): lax.all_gather(both, axis, axis=dim, tiled=True)  173 us
    reduce_scatter x1, waiting for transfers between devices, local(): lax.psum_scatter(jnp.einsum('rc,rh->ch', grad_all, activated, preferred_e...  109 us
    reduce_scatter x1, waiting for transfers between devices, local(): lax.psum_scatter(branch.astype(jnp.bfloat16), TENSOR, scatter_dimension=0...  84.2 us
    all_gather x2, waiting for transfers between devices, all_blocks(): tiles = lax.all_gather(tiles, axes[k])  53.9 us
    all_gather x2, blocking collectives, all_blocks(): tiles = lax.all_gather(tiles, axes[k])  38.4 us
    all_to_all x1, starting transfers between devices, copy_for_each(): lax.all_to_all(jnp.broadcast_to(array[None], (devices, *array.shape)), ax...  23.1 us
    all_to_all x1, blocking collectives, side_by_side(): lax.all_to_all(both, axis, split_axis=split_dim, concat_axis=concat_dim,...  22.6 us
    all_to_all x1, blocking collectives, regroup_rows(): lax.all_to_all(payload[0], ('group', 'dp'), split_axis=1, concat_axis=1,...  19.3 us
  transfers between devices with their start and end apart: 8, of which 6 were waited for; matrix products, arithmetic and copies ran while one was open for 5% of the time, Pallas kernels for 0%

profile of v1, /device:TPU:8, one launch (start us, length us, event | category | flops | bytes accessed | tf_op | source)
XLA Modules:
  0.0 604.7 jit_solution(16531037088608596531)
XLA Ops:
  8.1 0.7 fusion.24
  8.8 0.8 select_reduce_fusion.1
  9.7 0.7 multiply_add_fusion
  10.3 0.9 select_reduce_fusion
  11.2 0.8 fusion.13
  12.1 0.1 copy.40
  12.2 1.2 fusion.4
  13.4 0.4 copy.55
  13.8 0.5 broadcast.103
  14.3 2.1 reduce.5
  16.4 0.1 reshape.172
  16.5 22.6 %all_to_all.21 = bf16[16,2,3585]{2,1,0:T(2,128)(2,1)S(1)} all-to-all(bf16[16,2,3585]{2,1,0:T(2,128)(2,1)S(1)} %reshape.172), channel_id=1, replica_groups=mesh['group'=2,'dp'=8,'tensor_0'=4,'tensor_1'=4] {'group','dp'}, dimensions={0} | all-to-all | bytes 458880 | tf_op jit(solution)/shard_map/all_to_all | solution.py:19
  39.2 0.2 reshape.173
  39.4 0.5 slice.16
  39.9 0.2 fusion.17
  40.1 0.1 fusion.19
  40.2 21.6 %all_gather.25 = bf16[4,32,3584]{2,1,0:T(8,128)(2,1)} all-gather(bf16[1,32,3584]{2,1,0:T(8,128)(2,1)S(1)} %fusion.19), channel_id=1, replica_groups=mesh['group'=2,'dp'=8,'tensor_0'=4,'tensor_1'=4] {'tensor_0'}, dimensions={0}, use_global_device_ids=true | all-gather | bytes 1146880 | tf_op jit(solution)/shard_map/all_gather | solution.py:50
  61.9 1.0 pad_maximum_fusion
  62.9 0.4 fusion.11
  63.3 0.3 copy.44
  63.6 19.3 %all_to_all.22 = bf16[16,32,512]{2,0,1:T(8,128)(2,1)S(1)} all-to-all(bf16[16,32,512]{2,0,1:T(8,128)(2,1)S(1)} %copy.44), channel_id=1, replica_groups=mesh['group'=2,'dp'=8,'tensor_0'=4,'tensor_1'=4] {'group','dp'}, dimensions={1} | all-to-all | bytes 1048576 | tf_op jit(solution)/shard_map/all_to_all | solution.py:95
  82.9 2.4 stack.2
  85.3 4.7 all-to-all-start.1
  90.1 0.3 copy_convert_fusion
  90.4 0.1 fusion.14
  90.5 6.0 convolution_convert_fusion.1
  96.6 0.2 reduce-scatter.4.cloned.1.call-start
  96.8 6.6 %all-gather.9.cloned.1.call-done = bf16[16,32,3584]{2,1,0:T(8,128)(2,1)} async-done(((bf16[4,32,3584]{2,1,0:T(8,128)(2,1)}), bf16[16,32,3584]{2,1,0:T(8,128)(2,1)}) %all-gather.9.cloned.1.call-update) | async-done | bytes 3670032 | tf_op jit(solution)/shard_map/all_gather | solution.py:50
  103.4 4.1 copy.43
  107.6 172.9 %all-gather.7.cloned.1.call-done = bf16[3584,1184]{1,0:T(8,128)(2,1)} async-done(((bf16[224,1184]{1,0:T(8,128)(2,1)}), bf16[3584,1184]{1,0:T(8,128)(2,1)}) %all-gather.7.cloned.1.call-update) | async-done | bytes 8486928 | tf_op jit(solution)/shard_map/all_gather | solution.py:63
  280.5 5.9 fusion.2
  286.5 1.2 copy-done.7
  287.6 4.2 fusion.8
  291.9 6.9 %convolution_convert_fusion.2 = bf16[512,3584]{1,0:T(8,128)(2,1)} fusion(bf16[512,592]{0,1:T(8,128)(2,1)S(1)} %fusion.8, bf16[592,3584]{0,1:T(8,128)(2,1)} %bitcast.12), kind=kOutput, calls=%fused_computation.2 | convolution fusion | flops 2174484480 | bytes 8519680 | tf_op jit(solution)/shard_map/dot_general | solution.py:178
  298.8 0.4 multiply_reduce_fusion
  299.1 0.1 broadcast_in_dim.23
  299.2 0.6 broadcast_in_dim.38
  299.9 23.1 %all-to-all-start.3 = ((f32[16,1,512]{2,1,0:T(1,128)}), f32[16,1,512]{2,1,0:T(1,128)S(1)}, u32[]{:S(2)}, u32[]{:S(2)}) async-start(f32[16,1,512]{2,1,0:T(1,128)} %broadcast_in_dim.38), calls=%async_computation.5 | async-start | bytes 65536 | tf_op jit(solution)/shard_map/all_to_all | solution.py:32
  323.0 0.3 fusion.22
  323.4 6.4 %all-to-all-done.3 = f32[16,1,512]{2,1,0:T(1,128)S(1)} async-done(((f32[16,1,512]{2,1,0:T(1,128)}), f32[16,1,512]{2,1,0:T(1,128)S(1)}, u32[]{:S(2)}, u32[]{:S(2)}) %all-to-all-start.3) | async-done | bytes 32800 | tf_op jit(solution)/shard_map/all_to_all | solution.py:32
  329.9 84.2 %reduce-scatter.4.cloned.1.call-done = bf16[32,3584]{1,0:T(8,128)(2,1)} async-done(((bf16[512,3584]{1,0:T(8,128)(2,1)}), bf16[32,3584]{1,0:T(8,128)(2,1)}) %reduce-scatter.4.cloned.1.call-update) | async-done | bytes 229392 | tf_op jit(solution)/shard_map/reduce_scatter | solution.py:181
  414.1 1.9 multiply_convert_fusion
  416.0 16.8 %all-gather.1 = bf16[128,3584]{1,0:T(8,128)(2,1)} all-gather(bf16[32,3584]{1,0:T(8,128)(2,1)S(1)} %get-tuple-element.4), channel_id=3, replica_groups=mesh['group'=2,'dp'=8,'tensor_0'=4,'tensor_1'=4] {'tensor_0'}, dimensions={0}, use_global_device_ids=true | all-gather | bytes 1146880 | tf_op jit(solution)/shard_map/all_gather | solution.py:50
  432.9 47.2 %all-gather.11.cloned.1.call-done = bf16[16,32,3584]{2,1,0:T(8,128)(2,1)} async-done(((bf16[4,32,3584]{2,1,0:T(8,128)(2,1)}), bf16[16,32,3584]{2,1,0:T(8,128)(2,1)}) %all-gather.11.cloned.1.call-update) | async-done | bytes 3670032 | tf_op jit(solution)/shard_map/all_gather | solution.py:50
  480.1 2.3 copy.47
  482.4 4.7 convolution_convert_fusion
  487.1 108.6 %reduce-scatter.8.cloned.1.call-done = bf16[224,592]{1,0:T(8,128)(2,1)} async-done(((bf16[3584,592]{1,0:T(8,128)(2,1)}), bf16[224,592]{1,0:T(8,128)(2,1)}) %reduce-scatter.8.cloned.1.call-update) | async-done | bytes 265232 | tf_op jit(solution)/shard_map/reduce_scatter | solution.py:191
  595.7 1.8 convert_element_type.128
  (34 shorter events, 0.5 us)
Async XLA Ops:
  8.0 54.9 %copy-start = (bf16[256,512]{1,0:T(8,128)(2,1)S(1)}, bf16[256,512]{1,0:T(8,128)(2,1)}, u32[]{:S(2)}) copy-start(bf16[256,512]{1,0:T(8,128)(2,1)} %param.12) | copy-start | bytes 786436
  8.0 32.1 %copy-start.5 = (f32[3584]{0:T(1024)S(1)}, f32[3584]{0:T(1024)}, u32[]{:S(2)}) copy-start(f32[3584]{0:T(1024)} %param.16) | copy-start | bytes 43012
  8.0 95.4 %all-gather.9.cloned.1.call-start = ((), (), s32[]{:S(2)}) async-start(), calls=%async_computation.11 | async-start | bytes 4587520 | tf_op jit(solution)/shard_map/all_gather | solution.py:50
  13.4 48.5 %copy-start.3 = (bf16[224,592]{1,0:T(8,128)(2,1)S(1)}, bf16[224,592]{1,0:T(8,128)(2,1)}, u32[]{:S(2)}) copy-start(bf16[224,592]{1,0:T(8,128)(2,1)} %param.18) | copy-start | bytes 795652
  13.4 48.5 %copy-start.4 = (bf16[224,592]{1,0:T(8,128)(2,1)S(1)}, bf16[224,592]{1,0:T(8,128)(2,1)}, u32[]{:S(2)}) copy-start(bf16[224,592]{1,0:T(8,128)(2,1)} %param.17) | copy-start | bytes 795652
  40.0 42.9 %copy-start.2 = (bf16[592,224]{0,1:T(8,128)(2,1)S(1)}, bf16[592,224]{0,1:T(8,128)(2,1)}, u32[]{:S(2)}) copy-start(bf16[592,224]{0,1:T(8,128)(2,1)} %param.19) | copy-start | bytes 795652
  61.8 218.7 %all-gather.7.cloned.1.call-start = ((), (), s32[]{:S(2)}) async-start(), calls=%async_computation.7 | async-start | bytes 9748480 | tf_op jit(solution)/shard_map/all_gather | solution.py:63
  85.3 5.1 copy-start.6
  85.3 206.5 %all-to-all-start.1 = ((bf16[16,592,224]{1,2,0:T(8,128)(2,1)}), bf16[16,592,224]{1,2,0:T(8,128)(2,1)}, u32[]{:S(2)}, u32[]{:S(2)}) async-start(bf16[16,592,224]{1,2,0:T(8,128)(2,1)} %stack.2), calls=%async_computation.1 | async-start | bytes 9175040 | tf_op jit(solution)/shard_map/all_to_all | solution.py:175
  90.0 239.9 %reduce-scatter.6.cloned.1.call-start = ((), (), s32[]{:S(2)}) async-start(), calls=%async_computation.9 | async-start | bytes 3899392 | tf_op jit(solution)/shard_map/reduce_scatter | solution.py:154
  96.6 317.5 %reduce-scatter.4.cloned.1.call-start = ((), (), s32[]{:S(2)}) async-start(), calls=%async_computation.8 | async-start | bytes 3899392 | tf_op jit(solution)/shard_map/reduce_scatter | solution.py:181
  280.5 6.0 copy-start.1
  280.5 7.1 %copy-start.7 = (bf16[3584,1184]{1,0:T(8,128)(2,1)S(1)}, bf16[3584,1184]{1,0:T(8,128)(2,1)}, u32[]{:S(2)}) copy-start(bf16[3584,1184]{1,0:T(8,128)(2,1)} %all-gather.7.cloned.1.call-done) | copy-start | bytes 25460740
  299.9 29.9 %all-to-all-start.3 = ((f32[16,1,512]{2,1,0:T(1,128)}), f32[16,1,512]{2,1,0:T(1,128)S(1)}, u32[]{:S(2)}, u32[]{:S(2)}) async-start(f32[16,1,512]{2,1,0:T(1,128)} %broadcast_in_dim.38), calls=%async_computation.5 | async-start | bytes 65536 | tf_op jit(solution)/shard_map/all_to_all | solution.py:32
  323.0 157.1 %all-gather.11.cloned.1.call-start = ((), (), s32[]{:S(2)}) async-start(), calls=%async_computation.12 | async-start | bytes 4587520 | tf_op jit(solution)/shard_map/all_gather | solution.py:50
  432.8 162.9 %reduce-scatter.8.cloned.1.call-start = ((), (), s32[]{:S(2)}) async-start(), calls=%async_computation.10 | async-start | bytes 4874240 | tf_op jit(solution)/shard_map/reduce_scatter | solution.py:191
Sparse Core Ops, SparseCore 0:
  62.0 41.4 all-gather.8
  106.7 173.7 all-gather.6
  432.9 47.1 all-gather.10
  487.2 108.4 reduce-scatter.7
Sparse Core Ops, SparseCore 1:
  96.7 225.7 reduce-scatter.5
  324.8 89.2 reduce-scatter.3
